TPU v7x, 32 devices: a whole 2x2x4 slice. The times are simulated.
32 devices in a mesh: tile: 4 (over z), src: 8 (over y, x, core).
Axes of the slice: x: 2, y: 2, z: 4, core: 2. Of those that a mesh axis runs over, the one named last changes fastest.
Arguments:
- permittivity: float32 [64, 16, 320], P(('tile', 'src')), may hold values from 1 to 2
- e_start: float32 [8, 3, 64, 16, 320], P('src', None, 'tile'), may hold values from -6 to 6
- h_start: float32 [8, 3, 64, 16, 320], P('src', None, 'tile'), may hold values from -6 to 6
- e_cotangent: float32 [8, 3, 64, 16, 320], P('src', None, 'tile'), may hold values from -6 to 6
- h_cotangent: float32 [8, 3, 64, 16, 320], P('src', None, 'tile'), may hold values from -6 to 6
Outputs:
- e_final: float32 [8, 3, 64, 16, 320], P('src', None, 'tile')
- gradient: float32 [64, 16, 320], P(('tile', 'src'))
All inputs are finite; a program needn't handle non-finite values.
Results may differ from a plain program's by a relative error of at most 0.00002.
Values sent between devices are 32-bit elements; how exact they have to be, the bound alone decides.
A program may use at most 64 MiB of HBM per device.

v0:
```python
import jax
import jax.numpy as jnp
from jax import lax
from jax.sharding import PartitionSpec as P

STEPS = 6


courant = 0.57


def passed_along(array, axis, by):
    length = lax.axis_size(axis)
    pairs = [(i, i + by) for i in range(length) if 0 <= i + by < length]
    return lax.ppermute(array, axis, pairs)


def ahead_local(field, axis):
    size = field.shape[axis]
    upper = lax.slice_in_dim(field, 1, size, axis=axis)
    zeros = jnp.zeros_like(lax.slice_in_dim(field, 0, 1, axis=axis))
    return jnp.concatenate([upper, zeros], axis) - field


def behind_local(field, axis):
    size = field.shape[axis]
    lower = lax.slice_in_dim(field, 0, size - 1, axis=axis)
    zeros = jnp.zeros_like(lax.slice_in_dim(field, 0, 1, axis=axis))
    return field - jnp.concatenate([zeros, lower], axis)


def curl_local(field, differ):
    return jnp.stack(
        [
            differ(field[2], 1) - differ(field[1], 2),
            differ(field[0], 2) - differ(field[2], 0),
            differ(field[1], 0) - differ(field[0], 1),
        ]
    )


def plane_mask(count, depth):
    first = lax.axis_index("tile") * count - depth
    planes = first + jnp.arange(count + 2 * depth, dtype=jnp.int32)
    total = count * lax.axis_size("tile")
    valid = jnp.logical_and(planes >= 0, planes < total)
    return valid.astype(jnp.float32)[:, None, None]


def add_term(term, shard_total, local_total):
    shard_total = shard_total + lax.psum_scatter(term, "src", scatter_dimension=0, tiled=True)
    return (shard_total, local_total)


def on_device(permittivity, e_start, h_start, e_cotangent, h_cotangent):
    window = lax.all_gather(permittivity, "src", axis=0, tiled=True)
    inverse = 1.0 / window
    count = window.shape[0]
    depth = STEPS
    efield = e_start[0]
    hfield = h_start[0]
    stored = []
    mask = plane_mask(count, depth)
    stacked = jnp.concatenate([efield, hfield, inverse[None]], 0)
    above = passed_along(stacked[:, :depth], "tile", -1)
    below = passed_along(stacked[:, count - depth :], "tile", 1)
    padded = jnp.concatenate([below, stacked, above], 1)
    e_pad = padded[0:3]
    h_pad = padded[3:6]
    inv_pad = padded[6]
    for turn in range(STEPS):
        h_pad = (h_pad - courant * curl_local(e_pad, ahead_local)) * mask
        curled_pad = curl_local(h_pad, behind_local)
        e_pad = (e_pad + courant * inv_pad * curled_pad) * mask
        stored.append(curled_pad[:, depth : depth + count])
    efield = e_pad[:, depth : depth + count]
    hfield = h_pad[:, depth : depth + count]
    adj_efield = e_cotangent[0]
    adj_hfield = h_cotangent[0]
    shard_total = jnp.zeros(permittivity.shape, jnp.float32)
    local_total = jnp.zeros(window.shape, jnp.float32)
    mask = plane_mask(count, depth)
    members = [adj_efield, adj_hfield, inverse[None]]
    stacked = jnp.concatenate(members, 0)
    above = passed_along(stacked[:, :depth], "tile", -1)
    below = passed_along(stacked[:, count - depth :], "tile", 1)
    padded = jnp.concatenate([below, stacked, above], 1)
    a_pad = padded[0:3]
    b_pad = padded[3:6]
    inv_pad = padded[6]
    e_pad = padded[7:10]
    h_pad = padded[10:13]
    for turn in range(STEPS - 1, -1, -1):
        curled = stored[turn]
        term = courant * jnp.sum(a_pad[:, depth : depth + count] * curled, axis=0)
        shard_total, local_total = add_term(term, shard_total, local_total)
        b_pad = (b_pad + courant * curl_local(inv_pad * a_pad, ahead_local)) * mask
        a_pad = (a_pad - courant * curl_local(b_pad, behind_local)) * mask
    gradient = -shard_total / (permittivity * permittivity)
    return (efield[None], gradient)


def solution(mesh):
    in_specs = (
        P(("tile", "src"), None, None),
        P("src", None, "tile", None, None),
        P("src", None, "tile", None, None),
        P("src", None, "tile", None, None),
        P("src", None, "tile", None, None),
    )
    out_specs = (P("src", None, "tile", None, None), P(("tile", "src"), None, None))
    return jax.shard_map(
        on_device, mesh=mesh, in_specs=in_specs, out_specs=out_specs, check_vma=False
    )
```

profile of v0, /device:TPU:0, one launch (start us, length us, event | category | flops | bytes accessed | tf_op | source)
XLA Modules:
  0.0 171.6 jit_solution(8257954732582646804)
XLA Ops:
  7.2 11.3 %all_gather.3 = f32[16,16,320]{2,1,0:T(8,128)S(1)} all-gather(f32[2,16,320]{2,1,0:T(8,128)} %param.5), channel_id=1, replica_groups=mesh['tile'=4,'src'=8] {'src'}, dimensions={0}, use_global_device_ids=true | all-gather | bytes 368640 | tf_op jit(solution)/shard_map/all_gather | solution.py:56
  18.6 3.0 %pad_maximum_fusion.2 = (f32[7,16,16,320]{3,2,1,0:T(8,128)S(1)}, f32[7,16,16,320]{3,2,1,0:T(8,128)S(1)}) fusion(f32[1,16,16,320]{3,2,1,0:T(8,128)S(1)} %divide_bitcast_fusion, f32[3,16,16,320]{3,2,1,0:T(8,128)} %bitcast.697, f32[3,16,16,320]{3,2,1,0:T(8,128)} %bitcast.673, f32[3,16,16,320]{3,2,1,0:T(8,128)} %bitcast.699, f32[3,16,16,320]{3,2,1,0:T(8,128)} %bitcast.701), kind=kLoop, calls=%fused_computation.6 | loop fusion | flops 2293760 | bytes 8847360 | tf_op jit(solution)/shard_map/concatenate | solution.py:84
  21.6 1.5 fusion.48
  23.0 4.4 %collective-permute-start.2 = (f32[7,6,16,320]{3,2,1,0:T(8,128)}, f32[7,6,16,320]{3,2,1,0:T(8,128)}, u32[]{:S(2)}, u32[]{:S(2)}) collective-permute-start(f32[7,6,16,320]{3,2,1,0:T(8,128)} %get-tuple-element.21), channel_id=1, source_target_pairs={{0,8},{8,16},{16,24},{1,9},{9,17},{17,25},{2,10},{10,18},{18,26},{... | collective-permute-start | bytes 2580488 | tf_op jit(solution)/shard_map/ppermute | solution.py:15
  27.5 1.3 collective-permute-start.3
  28.8 1.5 fusion.49
  30.3 5.6 %collective-permute-start = (f32[7,6,16,320]{3,2,1,0:T(8,128)}, f32[7,6,16,320]{3,2,1,0:T(8,128)}, u32[]{:S(2)}, u32[]{:S(2)}) collective-permute-start(f32[7,6,16,320]{3,2,1,0:T(8,128)} %get-tuple-element.23), channel_id=1, source_target_pairs={{0,8},{8,16},{16,24},{1,9},{9,17},{17,25},{2,10},{10,18},{18,26},{... | collective-permute-start | bytes 2580488 | tf_op jit(solution)/shard_map/ppermute | solution.py:15
  35.9 1.3 collective-permute-start.1
  37.2 0.6 slice.1288
  37.8 12.1 %collective-permute-done.2 = f32[7,6,16,320]{3,2,1,0:T(8,128)} collective-permute-done((f32[7,6,16,320]{3,2,1,0:T(8,128)}, f32[7,6,16,320]{3,2,1,0:T(8,128)}, u32[]{:S(2)}, u32[]{:S(2)}) %collective-permute-start.2) | collective-permute-done | bytes 860192 | tf_op jit(solution)/shard_map/ppermute | solution.py:15
  50.0 5.4 %collective-permute-done.3 = f32[7,6,16,320]{3,2,1,0:T(8,128)} collective-permute-done((f32[7,6,16,320]{3,2,1,0:T(8,128)}, f32[7,6,16,320]{3,2,1,0:T(8,128)}, u32[]{:S(2)}, u32[]{:S(2)}) %collective-permute-start.3) | collective-permute-done | bytes 860192 | tf_op jit(solution)/shard_map/ppermute | solution.py:15
  55.3 16.2 %collective-permute-done = f32[7,6,16,320]{3,2,1,0:T(8,128)} collective-permute-done((f32[7,6,16,320]{3,2,1,0:T(8,128)}, f32[7,6,16,320]{3,2,1,0:T(8,128)}, u32[]{:S(2)}, u32[]{:S(2)}) %collective-permute-start) | collective-permute-done | bytes 860192 | tf_op jit(solution)/shard_map/ppermute | solution.py:15
  71.5 5.1 %collective-permute-done.1 = f32[7,6,16,320]{3,2,1,0:T(8,128)} collective-permute-done((f32[7,6,16,320]{3,2,1,0:T(8,128)}, f32[7,6,16,320]{3,2,1,0:T(8,128)}, u32[]{:S(2)}, u32[]{:S(2)}) %collective-permute-start.1) | collective-permute-done | bytes 860192 | tf_op jit(solution)/shard_map/ppermute | solution.py:15
  76.6 3.2 %fusion.3 = (f32[7,28,16,320]{3,2,1,0:T(8,128)S(1)}, f32[7,28,16,320]{3,2,1,0:T(8,128)S(1)}) fusion(f32[1,16,16,320]{3,2,1,0:T(8,128)} %copy-done.6, f32[7,6,16,320]{3,2,1,0:T(8,128)} %collective-permute-done.3, f32[3,16,16,320]{3,2,1,0:T(8,128)S(1)} %bitcast.698, f32[3,16,16,320]{3,2,1,0:T(8,128)S(1)} %bitcast.674, ...), kind=kLoop, calls=%fused_computation.5 | loop fusion | flops 8028160 | bytes 15728640 | tf_op jit(solution)/shard_map/concatenate | solution.py:87
  79.9 0.3 slice_bitcast_fusion.66
  81.6 0.5 subtract_bitcast_fusion.29
  82.1 0.3 fusion.4
  82.6 0.7 subtract_bitcast_fusion.26
  83.4 0.5 broadcast_multiply_fusion.3
  84.7 0.5 subtract_bitcast_fusion.23
  85.2 0.5 fusion.20
  86.0 0.7 subtract_bitcast_fusion.20
  86.7 0.5 broadcast_multiply_fusion.2
  88.0 0.5 subtract_bitcast_fusion.17
  88.5 0.9 fusion.24
  89.6 0.7 subtract_bitcast_fusion.14
  90.4 0.5 broadcast_multiply_fusion.1
  92.0 0.4 subtract_bitcast_fusion.65
  92.4 0.5 subtract_bitcast_fusion.11
  92.9 1.5 fusion.28
  94.9 0.8 slice.1285
  95.7 0.7 subtract_bitcast_fusion.8
  96.4 0.7 subtract_bitcast_fusion.62
  97.1 2.5 %pad_maximum_fusion.4 = (f32[3,28,16,320]{3,2,1,0:T(8,128)}, f32[3,28,16,320]{3,2,1,0:T(8,128)S(1)}, f32[3,28,16,320]{3,2,1,0:T(8,128)S(1)}, f32[3,28,16,320]{3,2,1,0:T(8,128)}) fusion(f32[1,28,16,320]{3,2,1,0:T(8,128)S(1)} %get-tuple-element.198, f32[1,28,16,320]{3,2,1,0:T(8,128)S(1)} %get-tuple-element.199, f32[1,28,16,320]{3,2,1,0:T(8,128)S(1)} %get-tuple-element.197, ...), kind=kLoop, calls=%fused_computation.15 | loop fusion | flops 4730880 | bytes 14909552 | tf_op jit(solution)/shard_map/stack | solution.py:33
  101.0 0.4 subtract_bitcast_fusion.59
  102.2 0.4 subtract_bitcast_fusion.5
  102.6 1.5 subtract_bitcast_fusion.56
  104.2 1.8 %pad_maximum_fusion.5 = (f32[3,28,16,320]{3,2,1,0:T(8,128)S(1)}, f32[3,28,16,320]{3,2,1,0:T(8,128)S(1)}, f32[3,28,16,320]{3,2,1,0:T(8,128)S(1)}) fusion(f32[1,28,16,320]{3,2,1,0:T(8,128)S(1)} %get-tuple-element.182, f32[1,28,16,320]{3,2,1,0:T(8,128)} %get-tuple-element.183, f32[1,28,16,320]{3,2,1,0:T(8,128)S(1)} %get-tuple-element.181, ...), kind=kLoop, calls=%fused_computation.19 | loop fusion | flops 4300800 | bytes 12615792 | tf_op jit(solution)/shard_map/stack | solution.py:33
  106.0 1.2 slice_bitcast_fusion.68
  107.2 1.0 slice_bitcast_fusion.2
  109.0 0.5 subtract_bitcast_fusion.53
  109.5 0.5 fusion.10
  110.3 0.8 subtract_bitcast_fusion.50
  111.1 0.5 pad_maximum_fusion.6
  112.5 0.5 subtract_bitcast_fusion.47
  113.0 1.1 fusion.12
  114.4 0.7 subtract_bitcast_fusion.44
  115.0 0.5 pad_maximum_fusion.7
  116.4 0.5 subtract_bitcast_fusion.41
  117.0 1.1 fusion.14
  118.3 0.8 subtract_bitcast_fusion.38
  119.1 0.5 pad_maximum_fusion.8
  120.5 0.6 subtract_bitcast_fusion.35
  121.1 1.5 fusion.16
  123.3 0.8 subtract_bitcast_fusion.32
  124.3 0.9 copy-done.7
  125.6 0.8 subtract_bitcast_fusion.2
  126.4 0.4 copy-done.1
  126.8 0.7 copy-done.2
  127.5 0.6 copy-done.3
  128.2 1.9 %multiply_reduce_fusion = (f32[16,16,320]{2,1,0:T(8,128)S(1)}, f32[1,3,16,16,320]{4,3,2,1,0:T(8,128)}, f32[16,16,320]{2,1,0:T(8,128)S(1)}, f32[16,16,320]{2,1,0:T(8,128)S(1)}) fusion(f32[3,28,16,320]{3,2,1,0:T(8,128)S(1)} %pad_maximum_fusion.9, f32[1,3,16,16,320]{4,3,2,1,0:T(8,128)S(1)} %copy-done.1, f32[16]{0:T(128)S(1)} %copy-done.12, ...), kind=kLoop, calls=%fused_computation.84 | loop fusion | flops 3194880 | bytes 9912384 | tf_op jit(solution)/shard_map/reduce_sum | solution.py:95
  130.1 1.0 add_multiply_fusion.4
  131.1 32.3 %reduce-scatter.2.cloned.1.call-done = f32[2,16,320]{2,1,0:T(8,128)} async-done(((f32[16,16,320]{2,1,0:T(8,128)}), f32[2,16,320]{2,1,0:T(8,128)}) %reduce-scatter.2.cloned.1.call-update) | async-done | bytes 40976 | tf_op jit(solution)/shard_map/reduce_scatter | solution.py:51
  163.4 1.4 multiply_divide_fusion
  (117 shorter events, 13.0 us)
Async XLA Ops:
  7.2 156.2 %reduce-scatter.2.cloned.1.call-start = ((), (), s32[]{:S(2)}) async-start(), calls=%async_computation.1 | async-start | bytes 442368 | tf_op jit(solution)/shard_map/reduce_scatter | solution.py:51
  18.6 4.5 %copy-start.6 = (f32[1,16,16,320]{3,2,1,0:T(8,128)}, f32[1,16,16,320]{3,2,1,0:T(8,128)S(1)}, u32[]{:S(2)}) copy-start(f32[1,16,16,320]{3,2,1,0:T(8,128)S(1)} %divide_bitcast_fusion) | copy-start | bytes 983044
  23.0 26.9 %collective-permute-start.2 = (f32[7,6,16,320]{3,2,1,0:T(8,128)}, f32[7,6,16,320]{3,2,1,0:T(8,128)}, u32[]{:S(2)}, u32[]{:S(2)}) collective-permute-start(f32[7,6,16,320]{3,2,1,0:T(8,128)} %get-tuple-element.21), channel_id=1, source_target_pairs={{0,8},{8,16},{16,24},{1,9},{9,17},{17,25},{2,10},{10,18},{18,26},{... | collective-permute-start | bytes 2580488 | tf_op jit(solution)/shard_map/ppermute | solution.py:15
  27.5 27.9 %collective-permute-start.3 = (f32[7,6,16,320]{3,2,1,0:T(8,128)}, f32[7,6,16,320]{3,2,1,0:T(8,128)}, u32[]{:S(2)}, u32[]{:S(2)}) collective-permute-start(f32[7,6,16,320]{3,2,1,0:T(8,128)} %get-tuple-element.22), channel_id=1, source_target_pairs={{8,0},{16,8},{24,16},{9,1},{17,9},{25,17},{10,2},{18,10},{26,18},{... | collective-permute-start | bytes 2580488 | tf_op jit(solution)/shard_map/ppermute | solution.py:15
  28.8 47.8 %copy-start = (f32[1,3,16,16,320]{4,3,2,1,0:T(8,128)S(1)}, f32[1,3,16,16,320]{4,3,2,1,0:T(8,128)}, u32[]{:S(2)}) copy-start(f32[1,3,16,16,320]{4,3,2,1,0:T(8,128)} %param.8) | copy-start | bytes 2949124
  28.8 47.8 %copy-start.4 = (f32[1,3,16,16,320]{4,3,2,1,0:T(8,128)S(1)}, f32[1,3,16,16,320]{4,3,2,1,0:T(8,128)}, u32[]{:S(2)}) copy-start(f32[1,3,16,16,320]{4,3,2,1,0:T(8,128)} %param.9) | copy-start | bytes 2949124
  28.8 47.8 %copy-start.5 = (f32[1,3,16,16,320]{4,3,2,1,0:T(8,128)S(1)}, f32[1,3,16,16,320]{4,3,2,1,0:T(8,128)}, u32[]{:S(2)}) copy-start(f32[1,3,16,16,320]{4,3,2,1,0:T(8,128)} %param.7) | copy-start | bytes 2949124
  30.3 41.2 %collective-permute-start = (f32[7,6,16,320]{3,2,1,0:T(8,128)}, f32[7,6,16,320]{3,2,1,0:T(8,128)}, u32[]{:S(2)}, u32[]{:S(2)}) collective-permute-start(f32[7,6,16,320]{3,2,1,0:T(8,128)} %get-tuple-element.23), channel_id=1, source_target_pairs={{0,8},{8,16},{16,24},{1,9},{9,17},{17,25},{2,10},{10,18},{18,26},{... | collective-permute-start | bytes 2580488 | tf_op jit(solution)/shard_map/ppermute | solution.py:15
  35.9 40.7 %collective-permute-start.1 = (f32[7,6,16,320]{3,2,1,0:T(8,128)}, f32[7,6,16,320]{3,2,1,0:T(8,128)}, u32[]{:S(2)}, u32[]{:S(2)}) collective-permute-start(f32[7,6,16,320]{3,2,1,0:T(8,128)} %get-tuple-element.24), channel_id=1, source_target_pairs={{8,0},{16,8},{24,16},{9,1},{17,9},{25,17},{10,2},{18,10},{26,18},{... | collective-permute-start | bytes 2580488 | tf_op jit(solution)/shard_map/ppermute | solution.py:15
  124.1 1.1 copy-start.7
  124.1 1.3 copy-start.8
  124.1 1.5 copy-start.9
  125.6 1.3 copy-start.1
  125.6 1.9 %copy-start.2 = (f32[3,28,16,320]{3,2,1,0:T(8,128)S(1)}, f32[3,28,16,320]{3,2,1,0:T(8,128)}, u32[]{:S(2)}) copy-start(f32[3,28,16,320]{3,2,1,0:T(8,128)} %get-tuple-element.49) | copy-start | bytes 5160964
  125.6 2.6 %copy-start.3 = (f32[3,28,16,320]{3,2,1,0:T(8,128)S(1)}, f32[3,28,16,320]{3,2,1,0:T(8,128)}, u32[]{:S(2)}) copy-start(f32[3,28,16,320]{3,2,1,0:T(8,128)} %get-tuple-element.211) | copy-start | bytes 5160964
  125.6 2.6 %copy-start.10 = (f32[16,16,320]{2,1,0:T(8,128)S(1)}, f32[16,16,320]{2,1,0:T(8,128)}, u32[]{:S(2)}) copy-start(f32[16,16,320]{2,1,0:T(8,128)} %slice.1285) | copy-start | bytes 983044
  125.6 2.6 %copy-start.12 = (f32[16]{0:T(128)S(1)}, f32[16]{0:T(128)}, u32[]{:S(2)}) copy-start(f32[16]{0:T(128)} %slice.1288) | copy-start | bytes 196
  130.1 33.3 %copy-start.11 = (f32[2,16,320]{2,1,0:T(8,128)S(1)}, f32[2,16,320]{2,1,0:T(8,128)}, u32[]{:S(2)}) copy-start(f32[2,16,320]{2,1,0:T(8,128)} %param.5) | copy-start | bytes 122884
Sparse Core Ops, SparseCore 0:
  131.2 32.1 reduce-scatter.1
where the time goes:
time: 172 us
  waiting for transfers between devices  71.1 us (41%)
  other arithmetic  40.8 us (24%)
  local copies, waits for them, and re-layouts  20.9 us (12%)
  between operations  14.9 us (9%)
  starting transfers between devices  12.7 us (7%)
  blocking collectives  11.3 us (7%)
    ppermute x4, waiting for transfers between devices, passed_along(): return lax.ppermute(array, axis, pairs)  38.8 us
    reduce_scatter x1, waiting for transfers between devices, add_term(): lax.psum_scatter(term, 'src', scatter_dimension=0, tiled=True)  32.3 us
    another operation x28, other arithmetic, curl_local(): jnp.stack([differ(field[2], 1) - differ(field[1], 2), differ(field[0], 2)...  20 us
    ppermute x4, starting transfers between devices, passed_along(): return lax.ppermute(array, axis, pairs)  12.6 us
    all_gather x1, blocking collectives, on_device(): window = lax.all_gather(permittivity, 'src', axis=0, tiled=True)  11.3 us
    slice x55, local copies, waits for them, and re-layouts, ahead_local(): upper = lax.slice_in_dim(field, 1, size, axis=axis)  7.54 us
    mul x8, other arithmetic, on_device(): b_pad = (b_pad + courant * curl_local(inv_pad * a_pad, ahead_local)) * mask  4.87 us
    mul x5, other arithmetic, on_device(): h_pad = (h_pad - courant * curl_local(e_pad, ahead_local)) * mask  4.47 us
  transfers between devices with their start and end apart: 5, of which 5 were waited for; matrix products, arithmetic and copies ran while one was open for 1% of the time, Pallas kernels for 0%

commit v1 on v0

v1 whole, which is shorter than its diff:
```python
import functools

import jax
import jax.numpy as jnp
from jax import lax
from jax.experimental import pallas as pl
from jax.experimental.pallas import tpu as pltpu
from jax.sharding import PartitionSpec as P

STEPS = 6
COURANT = 0.57
LANES = 128
ROWS = 8
MESH = pl.DeviceIdType.MESH


def group_of(total, most):
    return max(g for g in range(1, most + 1) if total % g == 0)


def over_planes(first, total, most, load, finish):
    group = group_of(total, most)

    def body(i, carry):
        base = first + i * group
        held = [load(base + j) for j in range(group)]
        for j in range(group):
            finish(base + j, held[j])
        return carry

    lax.fori_loop(0, total // group, body, 0)


def ahead_y(x):
    ny = x.shape[0]
    r = pltpu.roll(x, ny - 1, 0)
    low = r[ny - ROWS :]
    row = lax.broadcasted_iota(jnp.int32, low.shape, 0)
    low = jnp.where(row == ROWS - 1, 0.0, low)
    return jnp.concatenate([r[: ny - ROWS], low], 0) if ny > ROWS else low


def behind_y(x):
    ny = x.shape[0]
    r = pltpu.roll(x, 1, 0)
    top = r[:ROWS]
    row = lax.broadcasted_iota(jnp.int32, top.shape, 0)
    top = jnp.where(row == 0, 0.0, top)
    return jnp.concatenate([top, r[ROWS:]], 0) if ny > ROWS else top


def ahead_z(x):
    return pltpu.roll(x, x.shape[1] - 1, 1)


def behind_z(x):
    r = pltpu.roll(x, 1, 1)
    first = r[:, :LANES]
    lane = lax.broadcasted_iota(jnp.int32, first.shape, 1)
    first = jnp.where(lane == 0, 0.0, first)
    return jnp.concatenate([first, r[:, LANES:]], 1) if x.shape[1] > LANES else first


def kernel(
    tiles, sources,
    perm_ref, e_ref, h_ref, a_ref, b_ref,
    eout_ref, grad_ref,
    perm_in, e_in, h_in, a_in, b_in, e_last,
    coef, efield, hfield, ufield, bfield, deltas, grad, parts,
    in_sem, out_sem, perm_send, perm_recv, grad_send, grad_recv, halo_send, halo_recv,
):
    count, ny, nz = perm_in.shape
    wide = coef.shape[2]
    whole = nz // LANES * LANES
    rows = perm_ref.shape[0]
    tile = lax.axis_index("tile")
    me = lax.axis_index("src")
    has_below = tile > 0
    has_above = tile < tiles - 1
    own = pl.ds(me * rows, rows)

    loads = [
        pltpu.make_async_copy(e_ref.at[0], e_in, in_sem.at[0]),
        pltpu.make_async_copy(h_ref.at[0], h_in, in_sem.at[1]),
        pltpu.make_async_copy(perm_ref, perm_in.at[own], in_sem.at[2]),
        pltpu.make_async_copy(a_ref.at[0], a_in, in_sem.at[3]),
        pltpu.make_async_copy(b_ref.at[0], b_in, in_sem.at[4]),
    ]
    for copy in loads:
        copy.start()

    nothing = jnp.zeros((ny, wide), jnp.float32)
    for c in range(3):
        efield[c, count] = nothing
        hfield[c, 0] = nothing
        bfield[c, 0] = nothing
        for t in range(STEPS):
            ufield[t, c, count] = nothing

    barrier = pltpu.get_barrier_semaphore()
    for d in range(1, sources):
        pl.semaphore_signal(
            barrier, 1, device_id={"tile": tile, "src": lax.rem(me + d, sources)}, device_id_type=MESH
        )

    @pl.when(has_below)
    def _():
        pl.semaphore_signal(barrier, 1, device_id={"tile": tile - 1, "src": me}, device_id_type=MESH)

    @pl.when(has_above)
    def _():
        pl.semaphore_signal(barrier, 1, device_id={"tile": tile + 1, "src": me}, device_id_type=MESH)

    ends = jnp.where(has_below, 1, 0) + jnp.where(has_above, 1, 0)
    pl.semaphore_wait(barrier, sources - 1 + ends)

    def perm_copy(d):
        return pltpu.make_async_remote_copy(
            src_ref=perm_ref,
            dst_ref=perm_in.at[own],
            send_sem=perm_send.at[d - 1],
            recv_sem=perm_recv.at[d - 1],
            device_id={"tile": tile, "src": lax.rem(me + d, sources)},
            device_id_type=MESH,
        )

    def pad(ref, index, value):
        if whole:
            ref[index + (slice(None), slice(0, whole))] = value[:, :whole]
        if whole < nz:
            ref[index + (slice(None), slice(whole, nz))] = value[:, whole:]
        if nz < wide:
            ref[index + (slice(None), slice(nz, wide))] = jnp.zeros((ny, wide - nz), jnp.float32)

    def down(ref, slot):
        return pltpu.make_async_remote_copy(
            src_ref=ref.at[pl.ds(1, 2), 0],
            dst_ref=ref.at[pl.ds(1, 2), count],
            send_sem=halo_send.at[slot],
            recv_sem=halo_recv.at[slot],
            device_id={"tile": tile - 1, "src": me},
            device_id_type=MESH,
        )

    def up(ref, slot):
        return pltpu.make_async_remote_copy(
            src_ref=ref.at[pl.ds(1, 2), count],
            dst_ref=ref.at[pl.ds(1, 2), 0],
            send_sem=halo_send.at[slot],
            recv_sem=halo_recv.at[slot],
            device_id={"tile": tile + 1, "src": me},
            device_id_type=MESH,
        )

    def send_down(ref, slot):
        @pl.when(has_below)
        def _():
            down(ref, slot).start()

    def sent_down(ref, slot):
        @pl.when(has_below)
        def _():
            down(ref, slot).wait_send()

    def got_down(ref, slot):
        @pl.when(has_above)
        def _():
            down(ref, slot).wait_recv()

    def send_up(ref, slot):
        @pl.when(has_above)
        def _():
            up(ref, slot).start()

    def sent_up(ref, slot):
        @pl.when(has_above)
        def _():
            up(ref, slot).wait_send()

    def got_up(ref, slot):
        @pl.when(has_below)
        def _():
            up(ref, slot).wait_recv()

    def new_h(es, hs):
        def run(p):
            e0, e1, e2 = es[0, p], es[1, p], es[2, p]
            n1, n2 = es[1, p + 1], es[2, p + 1]
            h0 = hs[0, p + 1] - ((ahead_y(e2) - e2) - (ahead_z(e1) - e1))
            h1 = hs[1, p + 1] - ((ahead_z(e0) - e0) - (n2 - e2))
            h2 = hs[2, p + 1] - ((n1 - e1) - (ahead_y(e0) - e0))
            return h0, h1, h2

        return run

    def put_h(hs):
        def run(p, new):
            for c in range(3):
                hs[c, p + 1] = new[c]

        return run

    def new_e(es, hs):
        def run(p):
            h0, h1, h2 = hs[0, p + 1], hs[1, p + 1], hs[2, p + 1]
            m1, m2 = hs[1, p], hs[2, p]
            k = coef[p]
            d0 = k * ((h2 - behind_y(h2)) - (h1 - behind_z(h1)))
            d1 = k * ((h0 - behind_z(h0)) - (h2 - m2))
            d2 = k * ((h1 - m1) - (h0 - behind_y(h0)))
            d = (d0, d1, d2)
            return d, tuple(es[c, p] + d[c] for c in range(3))

        return run

    half = STEPS // 2

    def dot(left, right, p):
        return left[0] * right[0, p] + left[1] * right[1, p] + left[2] * right[2, p]

    def put_forward(t):
        def run(p, new):
            d, e = new
            if t == STEPS:
                for c in range(3):
                    e_last[c, p] = e[c][:, :nz]
            else:
                for c in range(3):
                    efield[c, p] = e[c]
            if t <= half:
                for c in range(3):
                    deltas[t, c, p] = d[c]
            else:
                grad[p] += dot(d, ufield.at[STEPS - t], p)

        return run

    def put_adjoint(t):
        def run(p, new):
            _, u = new
            if t < STEPS - 1:
                for c in range(3):
                    ufield[t, c, p] = u[c]
            if t >= half:
                term = dot(u, deltas.at[STEPS - t], p)
                grad[p] = term if t == half else grad[p] + term

        return run

    MOST = 5

    def h_inner(es, hs):
        over_planes(0, count - 1, MOST, new_h(es, hs), put_h(hs))

    def h_edge(es, hs):
        put_h(hs)(count - 1, new_h(es, hs)(count - 1))

    def e_inner(es, hs, put):
        over_planes(1, count - 1, MOST, new_e(es, hs), put)

    def e_edge(es, hs, put):
        put(0, new_e(es, hs)(0))

    loads[0].wait()

    def prepare_e(p):
        return tuple(e_in[c, p] for c in range(3))

    def finish_e(p, planes):
        for c in range(3):
            pad(efield, (c, p), planes[c])

    over_planes(0, count, 2, prepare_e, finish_e)
    send_down(efield, 0)
    for d in range(1, sources):
        perm_copy(d).start()
    loads[1].wait()

    def prepare_h(p):
        return tuple(h_in[c, p] * (1.0 / COURANT) for c in range(3))

    def finish_h(p, planes):
        for c in range(3):
            pad(hfield, (c, p + 1), planes[c])

    over_planes(0, count, 2, prepare_h, finish_h)
    h_inner(efield, hfield)
    got_down(efield, 0)
    h_edge(efield, hfield)
    send_up(hfield, 1)

    loads[4].wait()

    def prepare_b(p):
        return tuple(b_in[c, p] * (-1.0 / COURANT) for c in range(3))

    def finish_b(p, planes):
        for c in range(3):
            pad(bfield, (c, p + 1), planes[c])

    over_planes(0, count, 2, prepare_b, finish_b)
    loads[2].wait()
    loads[3].wait()
    for d in range(1, sources):
        perm_copy(d).wait_recv()

    def prepare_u(p):
        inverse = 1.0 / perm_in[p]
        return inverse * (COURANT * COURANT), tuple(inverse * a_in[c, p] for c in range(3))

    def finish_u(p, planes):
        k, u = planes
        pad(coef, (p,), k)
        for c in range(3):
            pad(ufield, (0, c, p), u[c])

    over_planes(0, count, 2, prepare_u, finish_u)
    send_down(ufield.at[0], 2)

    def grad_copy(d):
        peer = lax.rem(me + d, sources)
        return pltpu.make_async_remote_copy(
            src_ref=grad.at[pl.ds(peer * rows, rows)],
            dst_ref=parts.at[d - 1],
            send_sem=grad_send.at[d - 1],
            recv_sem=grad_recv.at[d - 1],
            device_id={"tile": tile, "src": peer},
            device_id_type=MESH,
        )

    for t in range(1, STEPS + 1):
        forward, adjoint = put_forward(t), put_adjoint(t)
        e_inner(efield, hfield, forward)
        if t < STEPS:
            h_inner(ufield.at[t - 1], bfield)
        else:
            for d in range(1, sources):
                @pl.when(lax.rem(me + d, sources) != 0)
                def _():
                    grad_copy(d).start()

            pltpu.make_async_copy(
                e_last.at[:, pl.ds(1, count - 1)], eout_ref.at[0, :, pl.ds(1, count - 1)], out_sem.at[0]
            ).start()
        got_up(hfield, 1)
        sent_down(efield, 0)
        e_edge(efield, hfield, forward)
        if t < STEPS:
            send_down(efield, 0)
            got_down(ufield.at[t - 1], 2)
            if t > 1:
                sent_up(bfield, 3)
            h_edge(ufield.at[t - 1], bfield)
            send_up(bfield, 3)
            sent_up(hfield, 1)
            h_inner(efield, hfield)
            e_inner(ufield.at[t - 1], bfield, adjoint) if t < STEPS else None
            got_down(efield, 0)
            h_edge(efield, hfield)
            send_up(hfield, 1)
            got_up(bfield, 3)
            e_edge(ufield.at[t - 1], bfield, adjoint)
            sent_down(ufield.at[t - 1], 2)
            if t < STEPS - 1:
                send_down(ufield.at[t], 2)

    for d in range(1, sources):
        @pl.when(lax.rem(me + d, sources) == 0)
        def _():
            grad_copy(d).start()

    tail = pltpu.make_async_copy(
        e_last.at[:, pl.ds(0, 1)], eout_ref.at[0, :, pl.ds(0, 1)], out_sem.at[1]
    )
    tail.start()
    sent_up(hfield, 1)
    sent_up(bfield, 3)
    total = grad[own]
    for d in range(1, sources):
        grad_copy(d).wait_recv()
        total = total + parts[d - 1]
    grad_ref[...] = -total[:, :, :nz]
    for d in range(1, sources):
        perm_copy(d).wait_send()
        grad_copy(d).wait_send()
    pltpu.make_async_copy(
        e_last.at[:, pl.ds(1, count - 1)], eout_ref.at[0, :, pl.ds(1, count - 1)], out_sem.at[0]
    ).wait()
    tail.wait()


def on_device(tiles, sources, permittivity, e_start, h_start, e_cotangent, h_cotangent):
    rows, ny, nz = permittivity.shape
    count = rows * sources
    wide = -(-nz // LANES) * LANES
    any_spec = pl.BlockSpec(memory_space=pl.ANY)
    vmem = lambda *shape: pltpu.VMEM(shape, jnp.float32)
    dma = lambda n: pltpu.SemaphoreType.DMA((n,))
    return pl.pallas_call(
        functools.partial(kernel, tiles, sources),
        out_shape=(
            jax.ShapeDtypeStruct(e_start.shape, jnp.float32),
            jax.ShapeDtypeStruct(permittivity.shape, jnp.float32),
        ),
        in_specs=[any_spec] * 5,
        out_specs=(any_spec, pl.BlockSpec(memory_space=pltpu.VMEM)),
        scratch_shapes=[
            vmem(count, ny, nz),
            vmem(3, count, ny, nz),
            vmem(3, count, ny, nz),
            vmem(3, count, ny, nz),
            vmem(3, count, ny, nz),
            vmem(3, count, ny, nz),
            vmem(count, ny, wide),
            vmem(3, count + 1, ny, wide),
            vmem(3, count + 1, ny, wide),
            vmem(STEPS, 3, count + 1, ny, wide),
            vmem(3, count + 1, ny, wide),
            vmem(STEPS // 2 + 1, 3, count, ny, wide),
            vmem(count, ny, wide),
            vmem(sources - 1, rows, ny, wide),
            dma(5),
            dma(2),
            dma(sources - 1),
            dma(sources - 1),
            dma(sources - 1),
            dma(sources - 1),
            dma(4),
            dma(4),
        ],
        compiler_params=pltpu.CompilerParams(
            collective_id=0, has_side_effects=True, vmem_limit_bytes=48 * 1024 * 1024
        ),
    )(permittivity, e_start, h_start, e_cotangent, h_cotangent)


def solution(mesh):
    fields = P("src", None, "tile", None, None)
    cells = P(("tile", "src"), None, None)
    return jax.shard_map(
        functools.partial(on_device, mesh.shape["tile"], mesh.shape["src"]),
        mesh=mesh,
        in_specs=(cells, fields, fields, fields, fields),
        out_specs=(fields, cells),
        check_vma=False,
    )
```

time: 172 us -> 57.6 us (0.33)
  waiting for transfers between devices: 71.1 us -> 0 us
  Pallas kernels: 0 us -> 49.2 us
  other arithmetic: 40.8 us -> 0 us
  between operations: 14.9 us -> 0.65 us
  local copies, waits for them, and re-layouts: 20.9 us -> 7.51 us
  starting transfers between devices: 12.7 us -> 0 us
  blocking collectives: 11.3 us -> 0 us
    pallas_call x0 -> x1, Pallas kernels: none -> 49.2 us  [on_device(): pl.pallas_call(functools.partial(kernel, tiles, sources), out_shape=(jax....]
    ppermute x4 -> x0, waiting for transfers between devices: 38.8 us -> none  [passed_along(): return lax.ppermute(array, axis, pairs)]
    reduce_scatter x1 -> x0, waiting for transfers between devices: 32.3 us -> none  [add_term(): lax.psum_scatter(term, 'src', scatter_dimension=0, tiled=True)]
    another operation x28 -> x0, other arithmetic: 20 us -> none  [curl_local(): jnp.stack([differ(field[2], 1) - differ(field[1], 2), differ(field[0], 2)...]
    slice x70 -> x0, local copies, waits for them, and re-layouts: 13.9 us -> none  [the longest x55 7.54 us: ahead_local(): upper = lax.slice_in_dim(field, 1, size, axis=axis)]
    ppermute x4 -> x0, starting transfers between devices: 12.6 us -> none  [passed_along(): return lax.ppermute(array, axis, pairs)]
    all_gather x1 -> x0, blocking collectives: 11.3 us -> none  [on_device(): window = lax.all_gather(permittivity, 'src', axis=0, tiled=True)]
    mul x13 -> x0, other arithmetic: 9.34 us -> none  [the longest x8 4.87 us: on_device(): b_pad = (b_pad + courant * curl_local(inv_pad * a_pad, ahead_local)) * mask]
  transfers between devices with their start and end apart: 5 -> 0, of which waited for: 5 -> 0; matrix products, arithmetic and copies ran while one was open for 1% -> 0% of each run, Pallas kernels for 0% -> 0%
where the time goes in v1:
time: 57.6 us; the launch traced here: 57.3 us
  Pallas kernels  49.2 us (85%)
  local copies, waits for them, and re-layouts  7.51 us (13%)
  between operations  0.65 us (1%)
    pallas_call x1, Pallas kernels, on_device(): pl.pallas_call(functools.partial(kernel, tiles, sources), out_shape=(jax....  49.2 us
    unnamed x12, local copies, waits for them, and re-layouts  7.51 us

profile of v1, /device:TPU:0, one launch (start us, length us, event | category | flops | bytes accessed | tf_op | source)
XLA Modules:
  0.0 57.3 jit_solution(13308600121580066845)
XLA Ops:
  0.6 0.0 copy-start
  0.6 1.3 %copy-done = f32[1,3,16,16,320]{4,3,2,1,0:T(8,128)S(1)} copy-done((f32[1,3,16,16,320]{4,3,2,1,0:T(8,128)S(1)}, f32[1,3,16,16,320]{4,3,2,1,0:T(8,128)}, u32[]{:S(2)}) %copy-start) | copy-done | bytes 983064
  1.9 0.0 copy-start.1
  1.9 1.3 %copy-done.1 = f32[1,3,16,16,320]{4,3,2,1,0:T(8,128)S(1)} copy-done((f32[1,3,16,16,320]{4,3,2,1,0:T(8,128)S(1)}, f32[1,3,16,16,320]{4,3,2,1,0:T(8,128)}, u32[]{:S(2)}) %copy-start.1) | copy-done | bytes 983064
  3.2 0.0 copy-start.2
  3.2 1.3 %copy-done.2 = f32[1,3,16,16,320]{4,3,2,1,0:T(8,128)S(1)} copy-done((f32[1,3,16,16,320]{4,3,2,1,0:T(8,128)S(1)}, f32[1,3,16,16,320]{4,3,2,1,0:T(8,128)}, u32[]{:S(2)}) %copy-start.2) | copy-done | bytes 983064
  4.4 0.0 copy-start.3
  4.4 1.3 %copy-done.3 = f32[1,3,16,16,320]{4,3,2,1,0:T(8,128)S(1)} copy-done((f32[1,3,16,16,320]{4,3,2,1,0:T(8,128)S(1)}, f32[1,3,16,16,320]{4,3,2,1,0:T(8,128)}, u32[]{:S(2)}) %copy-start.3) | copy-done | bytes 983064
  5.7 0.0 copy-start.4
  5.7 0.8 %copy-done.4 = f32[2,16,320]{2,1,0:T(8,128)S(1)} copy-done((f32[2,16,320]{2,1,0:T(8,128)S(1)}, f32[2,16,320]{2,1,0:T(8,128)}, u32[]{:S(2)}) %copy-start.4) | copy-done | bytes 40984
  6.5 49.2 %shard_map.68 = (f32[1,3,16,16,320]{4,3,2,1,0:T(8,128)S(1)}, f32[2,16,320]{2,1,0:T(8,128)S(1)}) custom-call(f32[2,16,320]{2,1,0:T(8,128)S(1)} %copy-done.4, f32[1,3,16,16,320]{4,3,2,1,0:T(8,128)S(1)} %copy-done, f32[1,3,16,16,320]{4,3,2,1,0:T(8,128)S(1)} %copy-done.1, f32[1,3,16,16,320]{4,3,2,1,0:T(8,128)S(1)} %copy-done.2, f32[1,3,16,16,320]{4,3,2,1,0:T(8,128)S(1)} %copy-done.3), custom_call_target="tpu_custom_call" | custom-call | tf_op jit(solution)/shard_map/pallas_call | solution.py:399
  55.7 1.0 %copy.9 = f32[1,3,16,16,320]{4,3,2,1,0:T(8,128)} copy(f32[1,3,16,16,320]{4,3,2,1,0:T(8,128)S(1)} %get-tuple-element.4) | data formatting | bytes 1966080
  56.7 0.6 %copy.10 = f32[2,16,320]{2,1,0:T(8,128)} copy(f32[2,16,320]{2,1,0:T(8,128)S(1)} %get-tuple-element.5) | data formatting | bytes 81920
Async XLA Ops:
  0.6 1.3 %copy-start = (f32[1,3,16,16,320]{4,3,2,1,0:T(8,128)S(1)}, f32[1,3,16,16,320]{4,3,2,1,0:T(8,128)}, u32[]{:S(2)}) copy-start(f32[1,3,16,16,320]{4,3,2,1,0:T(8,128)} %e_ref.1) | copy-start | bytes 2949124
  1.9 1.3 %copy-start.1 = (f32[1,3,16,16,320]{4,3,2,1,0:T(8,128)S(1)}, f32[1,3,16,16,320]{4,3,2,1,0:T(8,128)}, u32[]{:S(2)}) copy-start(f32[1,3,16,16,320]{4,3,2,1,0:T(8,128)} %h_ref.1) | copy-start | bytes 2949124
  3.2 1.3 %copy-start.2 = (f32[1,3,16,16,320]{4,3,2,1,0:T(8,128)S(1)}, f32[1,3,16,16,320]{4,3,2,1,0:T(8,128)}, u32[]{:S(2)}) copy-start(f32[1,3,16,16,320]{4,3,2,1,0:T(8,128)} %a_ref.1) | copy-start | bytes 2949124
  4.4 1.3 %copy-start.3 = (f32[1,3,16,16,320]{4,3,2,1,0:T(8,128)S(1)}, f32[1,3,16,16,320]{4,3,2,1,0:T(8,128)}, u32[]{:S(2)}) copy-start(f32[1,3,16,16,320]{4,3,2,1,0:T(8,128)} %b_ref.1) | copy-start | bytes 2949124
  5.7 0.8 %copy-start.4 = (f32[2,16,320]{2,1,0:T(8,128)S(1)}, f32[2,16,320]{2,1,0:T(8,128)}, u32[]{:S(2)}) copy-start(f32[2,16,320]{2,1,0:T(8,128)} %perm_ref.1) | copy-start | bytes 122884

commit v2 on v1

v2 whole, which is shorter than its diff:
```python
import functools

import jax
import jax.numpy as jnp
from jax import lax
from jax.experimental import pallas as pl
from jax.experimental.pallas import tpu as pltpu
from jax.sharding import PartitionSpec as P

STEPS = 6
COURANT = 0.57
LANES = 128
ROWS = 8
MESH = pl.DeviceIdType.MESH


def group_of(total, most):
    return max(g for g in range(1, most + 1) if total % g == 0)


def over_planes(first, total, most, run):
    group = group_of(total, most)

    def body(i, carry):
        run(first + i * group, group)
        return carry

    lax.fori_loop(0, total // group, body, 0)


def ahead_y(x):
    ny = x.shape[0]
    r = pltpu.roll(x, ny - 1, 0)
    low = r[ny - ROWS :]
    row = lax.broadcasted_iota(jnp.int32, low.shape, 0)
    low = jnp.where(row == ROWS - 1, 0.0, low)
    return jnp.concatenate([r[: ny - ROWS], low], 0) if ny > ROWS else low


def behind_y(x):
    ny = x.shape[0]
    r = pltpu.roll(x, 1, 0)
    top = r[:ROWS]
    row = lax.broadcasted_iota(jnp.int32, top.shape, 0)
    top = jnp.where(row == 0, 0.0, top)
    return jnp.concatenate([top, r[ROWS:]], 0) if ny > ROWS else top


def ahead_z(x):
    return pltpu.roll(x, x.shape[1] - 1, 1)


def behind_z(x):
    r = pltpu.roll(x, 1, 1)
    first = r[:, :LANES]
    lane = lax.broadcasted_iota(jnp.int32, first.shape, 1)
    first = jnp.where(lane == 0, 0.0, first)
    return jnp.concatenate([first, r[:, LANES:]], 1) if x.shape[1] > LANES else first


def kernel(
    tiles, sources,
    perm_ref, e_ref, h_ref, a_ref, b_ref,
    eout_ref, grad_ref,
    perm_in, e_in, h_in, a_in, b_in, e_last,
    coef, efield, hfield, ufield, bfield, halos, deltas, grad, parts,
    in_sem, out_sem, perm_send, perm_recv, grad_send, grad_recv, halo_send, halo_recv,
):
    count, ny, nz = perm_in.shape
    wide = coef.shape[2]
    whole = nz // LANES * LANES
    rows = perm_ref.shape[0]
    tile = lax.axis_index("tile")
    me = lax.axis_index("src")
    has_below = tile > 0
    has_above = tile < tiles - 1
    own = pl.ds(me * rows, rows)

    loads = [
        pltpu.make_async_copy(e_ref.at[0], e_in, in_sem.at[0]),
        pltpu.make_async_copy(h_ref.at[0], h_in, in_sem.at[1]),
        pltpu.make_async_copy(perm_ref, perm_in.at[own], in_sem.at[2]),
        pltpu.make_async_copy(a_ref.at[0], a_in, in_sem.at[3]),
        pltpu.make_async_copy(b_ref.at[0], b_in, in_sem.at[4]),
    ]
    for copy in loads:
        copy.start()

    nothing = jnp.zeros((ny, wide), jnp.float32)
    for c in range(3):
        efield[c, count] = nothing
        hfield[c, 0] = nothing
        bfield[c, 0] = nothing
        for t in range(STEPS):
            ufield[t, c, count] = nothing

    barrier = pltpu.get_barrier_semaphore()
    for d in range(1, sources):
        pl.semaphore_signal(
            barrier, 1, device_id={"tile": tile, "src": lax.rem(me + d, sources)}, device_id_type=MESH
        )

    @pl.when(has_below)
    def _():
        pl.semaphore_signal(barrier, 1, device_id={"tile": tile - 1, "src": me}, device_id_type=MESH)

    @pl.when(has_above)
    def _():
        pl.semaphore_signal(barrier, 1, device_id={"tile": tile + 1, "src": me}, device_id_type=MESH)

    ends = jnp.where(has_below, 1, 0) + jnp.where(has_above, 1, 0)
    pl.semaphore_wait(barrier, sources - 1 + ends)

    def perm_copy(d):
        return pltpu.make_async_remote_copy(
            src_ref=perm_ref,
            dst_ref=perm_in.at[own],
            send_sem=perm_send.at[d - 1],
            recv_sem=perm_recv.at[d - 1],
            device_id={"tile": tile, "src": lax.rem(me + d, sources)},
            device_id_type=MESH,
        )

    for d in range(1, sources):
        perm_copy(d).start()

    def pad(ref, index, value):
        if whole:
            ref[index + (slice(None), slice(0, whole))] = value[:, :whole]
        if whole < nz:
            ref[index + (slice(None), slice(whole, nz))] = value[:, whole:]
        if nz < wide:
            ref[index + (slice(None), slice(nz, wide))] = jnp.zeros((ny, wide - nz), jnp.float32)

    def down(ref, slot, c):
        return pltpu.make_async_remote_copy(
            src_ref=ref.at[c, 0],
            dst_ref=halos.at[slot, c - 1],
            send_sem=halo_send.at[slot, c - 1],
            recv_sem=halo_recv.at[slot, c - 1],
            device_id={"tile": tile - 1, "src": me},
            device_id_type=MESH,
        )

    def up(ref, slot, c):
        return pltpu.make_async_remote_copy(
            src_ref=ref.at[c, count],
            dst_ref=halos.at[slot, c - 1],
            send_sem=halo_send.at[slot, c - 1],
            recv_sem=halo_recv.at[slot, c - 1],
            device_id={"tile": tile + 1, "src": me},
            device_id_type=MESH,
        )

    def send_down(ref, slot, c):
        @pl.when(has_below)
        def _():
            down(ref, slot, c).start()

    def send_up(ref, slot, c):
        @pl.when(has_above)
        def _():
            up(ref, slot, c).start()

    def sent_down(ref, slot):
        @pl.when(has_below)
        def _():
            for c in (2, 1):
                down(ref, slot, c).wait_send()

    def sent_up(ref, slot):
        @pl.when(has_above)
        def _():
            for c in (1, 2):
                up(ref, slot, c).wait_send()

    def step_h(es, hs):
        def run(base, group):
            e0, e1, e2 = es[0, base], es[1, base], es[2, base]
            for j in range(group):
                p = base + j
                n1, n2 = es[1, p + 1], es[2, p + 1]
                hs[0, p + 1] -= (ahead_y(e2) - e2) - (ahead_z(e1) - e1)
                hs[1, p + 1] -= (ahead_z(e0) - e0) - (n2 - e2)
                hs[2, p + 1] -= (n1 - e1) - (ahead_y(e0) - e0)
                e1, e2 = n1, n2
                if j < group - 1:
                    e0 = es[0, p + 1]

        over_planes(0, count, MOST, run)

    def edge_h(es, hs, slot_in, slot_out):
        for c, other, sign in ((1, 2, 1.0), (2, 1, -1.0)):
            @pl.when(has_above)
            def _():
                down(es, slot_in, other).wait_recv()
                hs[c, count] += sign * halos[slot_in, other - 1]

            send_up(hs, slot_out, c)

    def step_e(hs, put):
        def run(base, group):
            m1, m2 = hs[1, base], hs[2, base]
            for p in [base + j for j in range(group)]:
                h0, h1, h2 = hs[0, p + 1], hs[1, p + 1], hs[2, p + 1]
                k = coef[p]
                put(
                    p,
                    (
                        k * ((h2 - behind_y(h2)) - (h1 - behind_z(h1))),
                        k * ((h0 - behind_z(h0)) - (h2 - m2)),
                        k * ((h1 - m1) - (h0 - behind_y(h0))),
                    ),
                )
                m1, m2 = h1, h2

        over_planes(0, count, MOST, run)

    def edge_e(hs, slot_in, fix, send):
        for c, other, sign in ((2, 1, -1.0), (1, 2, 1.0)):
            @pl.when(has_below)
            def _():
                up(hs, slot_in, other).wait_recv()
                fix(c, sign * (coef[0] * halos[slot_in, other - 1]))

            send(c)

    half = STEPS // 2

    def dot(left, right, p):
        return left[0] * right[0, p] + left[1] * right[1, p] + left[2] * right[2, p]

    def forward(t):
        def put(p, d):
            for c in range(3):
                if t == STEPS:
                    e_last[c, p] = (efield[c, p] + d[c])[:, :nz]
                else:
                    efield[c, p] += d[c]
                if t <= half:
                    deltas[t, c, p] = d[c]
            if t > half:
                grad[p] += dot(d, ufield.at[STEPS - t], p)

        def fix(c, d):
            if t == STEPS:
                e_last[c, 0] += d[:, :nz]
            else:
                efield[c, 0] += d
            if t <= half:
                deltas[t, c, 0] += d
            else:
                grad[0] += d * ufield[STEPS - t, c, 0]

        return put, fix

    def adjoint(t):
        def put(p, d):
            u = tuple(ufield[t - 1, c, p] + d[c] for c in range(3))
            if t < STEPS - 1:
                for c in range(3):
                    ufield[t, c, p] = u[c]
            if t >= half:
                term = dot(u, deltas.at[STEPS - t], p)
                grad[p] = term if t == half else grad[p] + term

        def fix(c, d):
            if t < STEPS - 1:
                ufield[t, c, 0] += d
            if t >= half:
                grad[0] += d * deltas[STEPS - t, c, 0]

        return put, fix

    MOST = 4

    loads[0].wait()

    def prepare_e(base, group):
        for p in [base + j for j in range(group)]:
            for c in range(3):
                pad(efield, (c, p), e_in[c, p])

    prepare_e(0, 1)
    for c in (2, 1):
        send_down(efield, 0, c)
    over_planes(1, count - 1, 3, prepare_e)
    loads[1].wait()

    def prepare_h(base, group):
        for p in [base + j for j in range(group)]:
            for c in range(3):
                pad(hfield, (c, p + 1), h_in[c, p] * (1.0 / COURANT))

    over_planes(0, count, 2, prepare_h)
    step_h(efield, hfield)
    edge_h(efield, hfield, 0, 1)

    loads[4].wait()

    def prepare_b(base, group):
        for p in [base + j for j in range(group)]:
            for c in range(3):
                pad(bfield, (c, p + 1), b_in[c, p] * (-1.0 / COURANT))

    over_planes(0, count, 2, prepare_b)
    loads[2].wait()
    loads[3].wait()
    for d in range(1, sources):
        perm_copy(d).wait_recv()

    def prepare_u(base, group):
        for p in [base + j for j in range(group)]:
            inverse = 1.0 / perm_in[p]
            pad(coef, (p,), inverse * (COURANT * COURANT))
            for c in range(3):
                pad(ufield, (0, c, p), inverse * a_in[c, p])

    prepare_u(0, 1)
    for c in (2, 1):
        send_down(ufield.at[0], 2, c)
    over_planes(1, count - 1, 3, prepare_u)

    def grad_copy(d):
        peer = lax.rem(me + d, sources)
        return pltpu.make_async_remote_copy(
            src_ref=grad.at[pl.ds(peer * rows, rows)],
            dst_ref=parts.at[d - 1],
            send_sem=grad_send.at[d - 1],
            recv_sem=grad_recv.at[d - 1],
            device_id={"tile": tile, "src": peer},
            device_id_type=MESH,
        )

    for t in range(1, STEPS + 1):
        last = t == STEPS
        before = ufield.at[t - 1]
        put, fix = forward(t)
        sent_down(efield, 0)
        step_e(hfield, put)
        if not last:
            if t > 1:
                sent_up(bfield, 3)
            step_h(before, bfield)
        else:
            for d in range(1, sources):
                @pl.when(lax.rem(me + d, sources) != 0)
                def _():
                    grad_copy(d).start()

            pltpu.make_async_copy(
                e_last.at[:, pl.ds(1, count - 1)], eout_ref.at[0, :, pl.ds(1, count - 1)], out_sem.at[0]
            ).start()
        edge_e(hfield, 1, fix, lambda c: None if last else send_down(efield, 0, c))
        if last:
            break
        edge_h(before, bfield, 2, 3)
        put, fix = adjoint(t)
        sent_up(hfield, 1)
        step_h(efield, hfield)
        sent_down(before, 2)
        step_e(bfield, put)
        edge_h(efield, hfield, 0, 1)
        edge_e(bfield, 3, fix, lambda c: send_down(ufield.at[t], 2, c) if t < STEPS - 1 else None)

    for d in range(1, sources):
        @pl.when(lax.rem(me + d, sources) == 0)
        def _():
            grad_copy(d).start()

    tail = pltpu.make_async_copy(
        e_last.at[:, pl.ds(0, 1)], eout_ref.at[0, :, pl.ds(0, 1)], out_sem.at[1]
    )
    tail.start()
    sent_up(hfield, 1)
    sent_up(bfield, 3)
    total = grad[own]
    for d in range(1, sources):
        grad_copy(d).wait_recv()
        total = total + parts[d - 1]
    grad_ref[...] = -total[:, :, :nz]
    for d in range(1, sources):
        perm_copy(d).wait_send()
        grad_copy(d).wait_send()
    pltpu.make_async_copy(
        e_last.at[:, pl.ds(1, count - 1)], eout_ref.at[0, :, pl.ds(1, count - 1)], out_sem.at[0]
    ).wait()
    tail.wait()


def on_device(tiles, sources, permittivity, e_start, h_start, e_cotangent, h_cotangent):
    rows, ny, nz = permittivity.shape
    count = rows * sources
    wide = -(-nz // LANES) * LANES
    any_spec = pl.BlockSpec(memory_space=pltpu.HBM)
    vmem = lambda *shape: pltpu.VMEM(shape, jnp.float32)
    dma = lambda n: pltpu.SemaphoreType.DMA((n,))
    return pl.pallas_call(
        functools.partial(kernel, tiles, sources),
        out_shape=(
            jax.ShapeDtypeStruct(e_start.shape, jnp.float32),
            jax.ShapeDtypeStruct(permittivity.shape, jnp.float32),
        ),
        in_specs=[any_spec] * 5,
        out_specs=(any_spec, pl.BlockSpec(memory_space=pltpu.VMEM)),
        scratch_shapes=[
            vmem(count, ny, nz),
            vmem(3, count, ny, nz),
            vmem(3, count, ny, nz),
            vmem(3, count, ny, nz),
            vmem(3, count, ny, nz),
            vmem(3, count, ny, nz),
            vmem(count, ny, wide),
            vmem(3, count + 1, ny, wide),
            vmem(3, count + 1, ny, wide),
            vmem(STEPS, 3, count + 1, ny, wide),
            vmem(3, count + 1, ny, wide),
            vmem(4, 2, ny, wide),
            vmem(STEPS // 2 + 1, 3, count, ny, wide),
            vmem(count, ny, wide),
            vmem(sources - 1, rows, ny, wide),
            dma(5),
            dma(2),
            dma(sources - 1),
            dma(sources - 1),
            dma(sources - 1),
            dma(sources - 1),
            pltpu.SemaphoreType.DMA((4, 2)),
            pltpu.SemaphoreType.DMA((4, 2)),
        ],
        compiler_params=pltpu.CompilerParams(
            collective_id=0, has_side_effects=True, vmem_limit_bytes=60 * 1024 * 1024
        ),
    )(permittivity, e_start, h_start, e_cotangent, h_cotangent)


def solution(mesh):
    fields = P("src", None, "tile", None, None)
    cells = P(("tile", "src"), None, None)
    return jax.shard_map(
        functools.partial(on_device, mesh.shape["tile"], mesh.shape["src"]),
        mesh=mesh,
        in_specs=(cells, fields, fields, fields, fields),
        out_specs=(fields, cells),
        check_vma=False,
    )
```

time: 57.6 us -> 49.7 us (0.86)
  local copies, waits for them, and re-layouts: 7.51 us -> 3 us
  Pallas kernels: 49.2 us -> 45.9 us
    unnamed x12 -> x4, local copies, waits for them, and re-layouts: 7.51 us -> 3 us
    pallas_call x1, Pallas kernels: 49.2 us -> 45.9 us  [on_device(): pl.pallas_call(functools.partial(kernel, tiles, sources), out_shape=(jax....]
where the time goes in v2:
time: 49.7 us; the launch traced here: 49.6 us
  Pallas kernels  45.9 us (92%)
  local copies, waits for them, and re-layouts  3 us (6%)
  between operations  0.65 us (1%)
    pallas_call x1, Pallas kernels, on_device(): pl.pallas_call(functools.partial(kernel, tiles, sources), out_shape=(jax....  45.9 us
    unnamed x4, local copies, waits for them, and re-layouts  3 us

profile of v2, /device:TPU:0, one launch (start us, length us, event | category | flops | bytes accessed | tf_op | source)
XLA Modules:
  0.0 49.6 jit_solution(11136575009829315954)
XLA Ops:
  0.6 45.9 %shard_map.68 = (f32[1,3,16,16,320]{4,3,2,1,0:T(8,128)}, f32[2,16,320]{2,1,0:T(8,128)}) custom-call(f32[2,16,320]{2,1,0:T(8,128)} %perm_ref.1, f32[1,3,16,16,320]{4,3,2,1,0:T(8,128)} %e_ref.1, f32[1,3,16,16,320]{4,3,2,1,0:T(8,128)} %h_ref.1, f32[1,3,16,16,320]{4,3,2,1,0:T(8,128)} %a_ref.1, f32[1,3,16,16,320]{4,3,2,1,0:T(8,128)} %b_ref.1), custom_call_target="tpu_custom_call" | custom-call | tf_op jit(solution)/shard_map/pallas_call | solution.py:398
  46.6 0.0 copy-start
  46.6 2.4 %copy.9 = f32[1,3,16,16,320]{4,3,2,1,0:T(8,128)} copy(f32[1,3,16,16,320]{4,3,2,1,0:T(8,128)} %get-tuple-element.4) | data formatting | bytes 1966080
  49.0 0.0 copy-done
  49.0 0.6 %copy.10 = f32[2,16,320]{2,1,0:T(8,128)} copy(f32[2,16,320]{2,1,0:T(8,128)S(1)} %copy-done) | data formatting | bytes 81920
Async XLA Ops:
  46.6 2.4 %copy-start = (f32[2,16,320]{2,1,0:T(8,128)S(1)}, f32[2,16,320]{2,1,0:T(8,128)}, u32[]{:S(2)}) copy-start(f32[2,16,320]{2,1,0:T(8,128)} %get-tuple-element.5) | copy-start | bytes 122884

commit v3 on v2

--- a/solution.py
+++ b/solution.py
@@ -28,34 +28,18 @@
     lax.fori_loop(0, total // group, body, 0)
 
 
-def ahead_y(x):
-    ny = x.shape[0]
-    r = pltpu.roll(x, ny - 1, 0)
-    low = r[ny - ROWS :]
-    row = lax.broadcasted_iota(jnp.int32, low.shape, 0)
-    low = jnp.where(row == ROWS - 1, 0.0, low)
-    return jnp.concatenate([r[: ny - ROWS], low], 0) if ny > ROWS else low
-
-
-def behind_y(x):
-    ny = x.shape[0]
-    r = pltpu.roll(x, 1, 0)
-    top = r[:ROWS]
-    row = lax.broadcasted_iota(jnp.int32, top.shape, 0)
-    top = jnp.where(row == 0, 0.0, top)
-    return jnp.concatenate([top, r[ROWS:]], 0) if ny > ROWS else top
-
-
 def ahead_z(x):
-    return pltpu.roll(x, x.shape[1] - 1, 1)
+    r = pltpu.roll(x, LANES - 1, 2)
+    after = jnp.concatenate([r[1:], jnp.zeros_like(r[:1])], 0)
+    lane = lax.broadcasted_iota(jnp.int32, r.shape, 2)
+    return jnp.where(lane == LANES - 1, after, r)
 
 
 def behind_z(x):
-    r = pltpu.roll(x, 1, 1)
-    first = r[:, :LANES]
-    lane = lax.broadcasted_iota(jnp.int32, first.shape, 1)
-    first = jnp.where(lane == 0, 0.0, first)
-    return jnp.concatenate([first, r[:, LANES:]], 1) if x.shape[1] > LANES else first
+    r = pltpu.roll(x, 1, 2)
+    before = jnp.concatenate([jnp.zeros_like(r[:1]), r[:-1]], 0)
+    lane = lax.broadcasted_iota(jnp.int32, r.shape, 2)
+    return jnp.where(lane == 0, before, r)
 
 
 def kernel(
@@ -67,8 +51,9 @@
     in_sem, out_sem, perm_send, perm_recv, grad_send, grad_recv, halo_send, halo_recv,
 ):
     count, ny, nz = perm_in.shape
-    wide = coef.shape[2]
-    whole = nz // LANES * LANES
+    chunks = coef.shape[1]
+    erows, hrows = pl.ds(0, ny), pl.ds(ROWS, ny)
+    eahead, hbehind = pl.ds(1, ny), pl.ds(ROWS - 1, ny)
     rows = perm_ref.shape[0]
     tile = lax.axis_index("tile")
     me = lax.axis_index("src")
@@ -86,13 +71,25 @@
     for copy in loads:
         copy.start()
 
-    nothing = jnp.zeros((ny, wide), jnp.float32)
-    for c in range(3):
-        efield[c, count] = nothing
-        hfield[c, 0] = nothing
-        bfield[c, 0] = nothing
-        for t in range(STEPS):
-            ufield[t, c, count] = nothing
+    nothing = jnp.zeros((chunks, ny, LANES), jnp.float32)
+    for c in (1, 2):
+        efield[c, count, :, erows] = nothing
+        hfield[c, 0, :, hrows] = nothing
+        bfield[c, 0, :, hrows] = nothing
+        for t in range(STEPS - 1):
+            ufield[t, c, count, :, erows] = nothing
+
+    def clear(p, carry):
+        margin = jnp.zeros((chunks, ROWS, LANES), jnp.float32)
+        for c in (0, 2):
+            efield[c, p, :, pl.ds(ny, ROWS)] = margin
+            hfield[c, p + 1, :, pl.ds(0, ROWS)] = margin
+            bfield[c, p + 1, :, pl.ds(0, ROWS)] = margin
+            for t in range(STEPS - 1):
+                ufield[t, c, p, :, pl.ds(ny, ROWS)] = margin
+        return carry
+
+    lax.fori_loop(0, count, clear, 0)
 
     barrier = pltpu.get_barrier_semaphore()
     for d in range(1, sources):
@@ -124,17 +121,23 @@
     for d in range(1, sources):
         perm_copy(d).start()
 
-    def pad(ref, index, value):
-        if whole:
-            ref[index + (slice(None), slice(0, whole))] = value[:, :whole]
-        if whole < nz:
-            ref[index + (slice(None), slice(whole, nz))] = value[:, whole:]
-        if nz < wide:
-            ref[index + (slice(None), slice(nz, wide))] = jnp.zeros((ny, wide - nz), jnp.float32)
+    def pad(ref, index, start, value):
+        for j in range(chunks):
+            part = value[:, j * LANES : (j + 1) * LANES]
+            have = part.shape[1]
+            at = index + (j, pl.ds(start, ny))
+            if have == LANES:
+                ref[at] = part
+            else:
+                ref[at + (pl.ds(0, have),)] = part
+                ref[at + (pl.ds(have, LANES - have),)] = jnp.zeros((ny, LANES - have), jnp.float32)
+
+    def unpad(value, j):
+        return value[..., : min(LANES, nz - j * LANES)]
 
     def down(ref, slot, c):
         return pltpu.make_async_remote_copy(
-            src_ref=ref.at[c, 0],
+            src_ref=ref.at[c, 0, :, erows],
             dst_ref=halos.at[slot, c - 1],
             send_sem=halo_send.at[slot, c - 1],
             recv_sem=halo_recv.at[slot, c - 1],
@@ -144,7 +147,7 @@
 
     def up(ref, slot, c):
         return pltpu.make_async_remote_copy(
-            src_ref=ref.at[c, count],
+            src_ref=ref.at[c, count, :, hrows],
             dst_ref=halos.at[slot, c - 1],
             send_sem=halo_send.at[slot, c - 1],
             recv_sem=halo_recv.at[slot, c - 1],
@@ -176,16 +179,15 @@
 
     def step_h(es, hs):
         def run(base, group):
-            e0, e1, e2 = es[0, base], es[1, base], es[2, base]
+            e1, e2 = es[1, base, :, erows], es[2, base, :, erows]
             for j in range(group):
                 p = base + j
-                n1, n2 = es[1, p + 1], es[2, p + 1]
-                hs[0, p + 1] -= (ahead_y(e2) - e2) - (ahead_z(e1) - e1)
-                hs[1, p + 1] -= (ahead_z(e0) - e0) - (n2 - e2)
-                hs[2, p + 1] -= (n1 - e1) - (ahead_y(e0) - e0)
+                e0 = es[0, p, :, erows]
+                n1, n2 = es[1, p + 1, :, erows], es[2, p + 1, :, erows]
+                hs[0, p + 1, :, hrows] -= (es[2, p, :, eahead] - e2) - (ahead_z(e1) - e1)
+                hs[1, p + 1, :, hrows] -= (ahead_z(e0) - e0) - (n2 - e2)
+                hs[2, p + 1, :, hrows] -= (n1 - e1) - (es[0, p, :, eahead] - e0)
                 e1, e2 = n1, n2
-                if j < group - 1:
-                    e0 = es[0, p + 1]
 
         over_planes(0, count, MOST, run)
 
@@ -194,22 +196,22 @@
             @pl.when(has_above)
             def _():
                 down(es, slot_in, other).wait_recv()
-                hs[c, count] += sign * halos[slot_in, other - 1]
+                hs[c, count, :, hrows] += sign * halos[slot_in, other - 1]
 
             send_up(hs, slot_out, c)
 
     def step_e(hs, put):
         def run(base, group):
-            m1, m2 = hs[1, base], hs[2, base]
+            m1, m2 = hs[1, base, :, hrows], hs[2, base, :, hrows]
             for p in [base + j for j in range(group)]:
-                h0, h1, h2 = hs[0, p + 1], hs[1, p + 1], hs[2, p + 1]
+                h0, h1, h2 = (hs[c, p + 1, :, hrows] for c in range(3))
                 k = coef[p]
                 put(
                     p,
                     (
-                        k * ((h2 - behind_y(h2)) - (h1 - behind_z(h1))),
+                        k * ((h2 - hs[2, p + 1, :, hbehind]) - (h1 - behind_z(h1))),
                         k * ((h0 - behind_z(h0)) - (h2 - m2)),
-                        k * ((h1 - m1) - (h0 - behind_y(h0))),
+                        k * ((h1 - m1) - (h0 - hs[0, p + 1, :, hbehind])),
                     ),
                 )
                 m1, m2 = h1, h2
@@ -227,46 +229,53 @@
 
     half = STEPS // 2
 
-    def dot(left, right, p):
-        return left[0] * right[0, p] + left[1] * right[1, p] + left[2] * right[2, p]
+    def dot(left, right):
+        return left[0] * right[0] + left[1] * right[1] + left[2] * right[2]
+
+    def put_last(c, p, value):
+        for j in range(chunks):
+            part = unpad(value[j], j)
+            e_last[c, p, :, pl.ds(j * LANES, part.shape[1])] = part
 
     def forward(t):
         def put(p, d):
             for c in range(3):
                 if t == STEPS:
-                    e_last[c, p] = (efield[c, p] + d[c])[:, :nz]
+                    put_last(c, p, efield[c, p, :, erows] + d[c])
                 else:
-                    efield[c, p] += d[c]
+                    efield[c, p, :, erows] += d[c]
                 if t <= half:
                     deltas[t, c, p] = d[c]
             if t > half:
-                grad[p] += dot(d, ufield.at[STEPS - t], p)
+                grad[p] += dot(d, [ufield[STEPS - t, c, p, :, erows] for c in range(3)])
 
         def fix(c, d):
             if t == STEPS:
-                e_last[c, 0] += d[:, :nz]
+                for j in range(chunks):
+                    part = unpad(d[j], j)
+                    e_last[c, 0, :, pl.ds(j * LANES, part.shape[1])] += part
             else:
-                efield[c, 0] += d
+                efield[c, 0, :, erows] += d
             if t <= half:
                 deltas[t, c, 0] += d
             else:
-                grad[0] += d * ufield[STEPS - t, c, 0]
+                grad[0] += d * ufield[STEPS - t, c, 0, :, erows]
 
         return put, fix
 
     def adjoint(t):
         def put(p, d):
-            u = tuple(ufield[t - 1, c, p] + d[c] for c in range(3))
+            u = tuple(ufield[t - 1, c, p, :, erows] + d[c] for c in range(3))
             if t < STEPS - 1:
                 for c in range(3):
-                    ufield[t, c, p] = u[c]
+                    ufield[t, c, p, :, erows] = u[c]
             if t >= half:
-                term = dot(u, deltas.at[STEPS - t], p)
+                term = dot(u, [deltas[STEPS - t, c, p] for c in range(3)])
                 grad[p] = term if t == half else grad[p] + term
 
         def fix(c, d):
             if t < STEPS - 1:
-                ufield[t, c, 0] += d
+                ufield[t, c, 0, :, erows] += d
             if t >= half:
                 grad[0] += d * deltas[STEPS - t, c, 0]
 
@@ -279,7 +288,7 @@
     def prepare_e(base, group):
         for p in [base + j for j in range(group)]:
             for c in range(3):
-                pad(efield, (c, p), e_in[c, p])
+                pad(efield, (c, p), 0, e_in[c, p])
 
     prepare_e(0, 1)
     for c in (2, 1):
@@ -290,7 +299,7 @@
     def prepare_h(base, group):
         for p in [base + j for j in range(group)]:
             for c in range(3):
-                pad(hfield, (c, p + 1), h_in[c, p] * (1.0 / COURANT))
+                pad(hfield, (c, p + 1), ROWS, h_in[c, p] * (1.0 / COURANT))
 
     over_planes(0, count, 2, prepare_h)
     step_h(efield, hfield)
@@ -301,7 +310,7 @@
     def prepare_b(base, group):
         for p in [base + j for j in range(group)]:
             for c in range(3):
-                pad(bfield, (c, p + 1), b_in[c, p] * (-1.0 / COURANT))
+                pad(bfield, (c, p + 1), ROWS, b_in[c, p] * (-1.0 / COURANT))
 
     over_planes(0, count, 2, prepare_b)
     loads[2].wait()
@@ -312,9 +321,9 @@
     def prepare_u(base, group):
         for p in [base + j for j in range(group)]:
             inverse = 1.0 / perm_in[p]
-            pad(coef, (p,), inverse * (COURANT * COURANT))
+            pad(coef, (p,), 0, inverse * (COURANT * COURANT))
             for c in range(3):
-                pad(ufield, (0, c, p), inverse * a_in[c, p])
+                pad(ufield, (0, c, p), 0, inverse * a_in[c, p])
 
     prepare_u(0, 1)
     for c in (2, 1):
@@ -334,7 +343,7 @@
 
     for t in range(1, STEPS + 1):
         last = t == STEPS
-        before = ufield.at[t - 1]
+        before = ufield.at[min(t, STEPS - 1) - 1]
         put, fix = forward(t)
         sent_down(efield, 0)
         step_e(hfield, put)
@@ -378,7 +387,9 @@
     for d in range(1, sources):
         grad_copy(d).wait_recv()
         total = total + parts[d - 1]
-    grad_ref[...] = -total[:, :, :nz]
+    for j in range(chunks):
+        part = unpad(total[:, j], j)
+        grad_ref[:, :, pl.ds(j * LANES, part.shape[2])] = -part
     for d in range(1, sources):
         perm_copy(d).wait_send()
         grad_copy(d).wait_send()
@@ -391,7 +402,7 @@
 def on_device(tiles, sources, permittivity, e_start, h_start, e_cotangent, h_cotangent):
     rows, ny, nz = permittivity.shape
     count = rows * sources
-    wide = -(-nz // LANES) * LANES
+    chunks = -(-nz // LANES)
     any_spec = pl.BlockSpec(memory_space=pltpu.HBM)
     vmem = lambda *shape: pltpu.VMEM(shape, jnp.float32)
     dma = lambda n: pltpu.SemaphoreType.DMA((n,))
@@ -410,15 +421,15 @@
             vmem(3, count, ny, nz),
             vmem(3, count, ny, nz),
             vmem(3, count, ny, nz),
-            vmem(count, ny, wide),
-            vmem(3, count + 1, ny, wide),
-            vmem(3, count + 1, ny, wide),
-            vmem(STEPS, 3, count + 1, ny, wide),
-            vmem(3, count + 1, ny, wide),
-            vmem(4, 2, ny, wide),
-            vmem(STEPS // 2 + 1, 3, count, ny, wide),
-            vmem(count, ny, wide),
-            vmem(sources - 1, rows, ny, wide),
+            vmem(count, chunks, ny, LANES),
+            vmem(3, count + 1, chunks, ny + ROWS, LANES),
+            vmem(3, count + 1, chunks, ny + ROWS, LANES),
+            vmem(STEPS - 1, 3, count + 1, chunks, ny + ROWS, LANES),
+            vmem(3, count + 1, chunks, ny + ROWS, LANES),
+            vmem(4, 2, chunks, ny, LANES),
+            vmem(STEPS // 2 + 1, 3, count, chunks, ny, LANES),
+            vmem(count, chunks, ny, LANES),
+            vmem(sources - 1, rows, chunks, ny, LANES),
             dma(5),
             dma(2),
             dma(sources - 1),

time: 49.7 us -> 49.7 us (level)
  no operation moved by 1% of the time
where the time goes in v3:
time: 49.7 us; the launch traced here: 49.5 us
  Pallas kernels  45.9 us (92%)
  local copies, waits for them, and re-layouts  3 us (6%)
  between operations  0.65 us (1%)
    pallas_call x1, Pallas kernels, on_device(): pl.pallas_call(functools.partial(kernel, tiles, sources), out_shape=(jax....  45.9 us
    unnamed x4, local copies, waits for them, and re-layouts  3 us

profile of v3, /device:TPU:0, one launch (start us, length us, event | category | flops | bytes accessed | tf_op | source)
XLA Modules:
  0.0 49.5 jit_solution(16032599951621092824)
XLA Ops:
  0.6 45.9 %shard_map.68 = (f32[1,3,16,16,320]{4,3,2,1,0:T(8,128)}, f32[2,16,320]{2,1,0:T(8,128)}) custom-call(f32[2,16,320]{2,1,0:T(8,128)} %perm_ref.1, f32[1,3,16,16,320]{4,3,2,1,0:T(8,128)} %e_ref.1, f32[1,3,16,16,320]{4,3,2,1,0:T(8,128)} %h_ref.1, f32[1,3,16,16,320]{4,3,2,1,0:T(8,128)} %a_ref.1, f32[1,3,16,16,320]{4,3,2,1,0:T(8,128)} %b_ref.1), custom_call_target="tpu_custom_call" | custom-call | tf_op jit(solution)/shard_map/pallas_call | solution.py:409
  46.5 0.0 copy-start
  46.5 2.4 %copy.9 = f32[1,3,16,16,320]{4,3,2,1,0:T(8,128)} copy(f32[1,3,16,16,320]{4,3,2,1,0:T(8,128)} %get-tuple-element.4) | data formatting | bytes 1966080
  48.9 0.0 copy-done
  48.9 0.6 %copy.10 = f32[2,16,320]{2,1,0:T(8,128)} copy(f32[2,16,320]{2,1,0:T(8,128)S(1)} %copy-done) | data formatting | bytes 81920
Async XLA Ops:
  46.5 2.4 %copy-start = (f32[2,16,320]{2,1,0:T(8,128)S(1)}, f32[2,16,320]{2,1,0:T(8,128)}, u32[]{:S(2)}) copy-start(f32[2,16,320]{2,1,0:T(8,128)} %get-tuple-element.5) | copy-start | bytes 122884

commit v4 on v3

--- a/solution.py
+++ b/solution.py
@@ -281,7 +281,7 @@
 
         return put, fix
 
-    MOST = 4
+    MOST = 8
 
     loads[0].wait()
 
@@ -399,6 +399,22 @@
     tail.wait()
 
 
+def hand_over(e_ref, grad_ref, eout_ref, gout_ref, sem):
+    first = e_ref.shape[2] // 2
+    copies = [pltpu.make_async_copy(grad_ref, gout_ref, sem.at[6])]
+    for c in range(3):
+        for i, planes in enumerate((pl.ds(0, first), pl.ds(first, e_ref.shape[2] - first))):
+            copies.append(
+                pltpu.make_async_copy(
+                    e_ref.at[0, c, planes], eout_ref.at[0, c, planes], sem.at[2 * c + i]
+                )
+            )
+    for copy in copies:
+        copy.start()
+    for copy in copies:
+        copy.wait()
+
+
 def on_device(tiles, sources, permittivity, e_start, h_start, e_cotangent, h_cotangent):
     rows, ny, nz = permittivity.shape
     count = rows * sources
@@ -406,7 +422,7 @@
     any_spec = pl.BlockSpec(memory_space=pltpu.HBM)
     vmem = lambda *shape: pltpu.VMEM(shape, jnp.float32)
     dma = lambda n: pltpu.SemaphoreType.DMA((n,))
-    return pl.pallas_call(
+    efinal, gradient = pl.pallas_call(
         functools.partial(kernel, tiles, sources),
         out_shape=(
             jax.ShapeDtypeStruct(e_start.shape, jnp.float32),
@@ -443,6 +459,18 @@
             collective_id=0, has_side_effects=True, vmem_limit_bytes=60 * 1024 * 1024
         ),
     )(permittivity, e_start, h_start, e_cotangent, h_cotangent)
+    hbm_spec = pl.BlockSpec(memory_space=pltpu.HBM)
+    return pl.pallas_call(
+        hand_over,
+        out_shape=(
+            jax.ShapeDtypeStruct(efinal.shape, jnp.float32),
+            jax.ShapeDtypeStruct(gradient.shape, jnp.float32),
+        ),
+        in_specs=[hbm_spec, hbm_spec],
+        out_specs=(hbm_spec, hbm_spec),
+        scratch_shapes=[dma(2 * 3 + 1)],
+        compiler_params=pltpu.CompilerParams(vmem_limit_bytes=60 * 1024 * 1024),
+    )(efinal, gradient)
 
 
 def solution(mesh):

time: 49.7 us -> 85.2 us (1.71)
  Pallas kernels: 45.9 us -> 84.4 us
  local copies, waits for them, and re-layouts: 3 us -> 0 us
    pallas_call x0 -> x1, Pallas kernels: none -> 38.4 us  [on_device(): pl.pallas_call(hand_over, out_shape=(jax.ShapeDtypeStruct(efinal.shape, j...]
    unnamed x4 -> x0, local copies, waits for them, and re-layouts: 3 us -> none
where the time goes in v4:
time: 85.2 us; the launch traced here: 85.1 us
  Pallas kernels  84.4 us (99%)
    pallas_call x1, Pallas kernels, on_device(): pl.pallas_call(functools.partial(kernel, tiles, sources), out_shape=(jax....  46 us
    pallas_call x1, Pallas kernels, on_device(): pl.pallas_call(hand_over, out_shape=(jax.ShapeDtypeStruct(efinal.shape, j...  38.4 us

profile of v4, /device:TPU:0, one launch (start us, length us, event | category | flops | bytes accessed | tf_op | source)
XLA Modules:
  0.0 85.1 jit_solution(17295822083243521995)
XLA Ops:
  0.6 46.0 %shard_map.68 = (f32[1,3,16,16,320]{4,3,2,1,0:T(8,128)}, f32[2,16,320]{2,1,0:T(8,128)}) custom-call(f32[2,16,320]{2,1,0:T(8,128)} %perm_ref.1, f32[1,3,16,16,320]{4,3,2,1,0:T(8,128)} %e_ref.1, f32[1,3,16,16,320]{4,3,2,1,0:T(8,128)} %h_ref.1, f32[1,3,16,16,320]{4,3,2,1,0:T(8,128)} %a_ref.1, f32[1,3,16,16,320]{4,3,2,1,0:T(8,128)} %b_ref.1), custom_call_target="tpu_custom_call" | custom-call | tf_op jit(solution)/shard_map/pallas_call | solution.py:425
  46.7 38.4 %shard_map.69 = (f32[1,3,16,16,320]{4,3,2,1,0:T(8,128)}, f32[2,16,320]{2,1,0:T(8,128)}) custom-call(f32[1,3,16,16,320]{4,3,2,1,0:T(8,128)} %get-tuple-element.4.e_ref, f32[2,16,320]{2,1,0:T(8,128)} %get-tuple-element.5.grad_ref), custom_call_target="tpu_custom_call" | custom-call | tf_op jit(solution)/shard_map/pallas_call | solution.py:463
